TPU v7x, 256 devices: a whole 4x4x8 slice. The times are simulated.
256 devices in a mesh: blk: 16 (over y_lo, z), grp: 16 (over y_hi, x, core).
Axes of the slice: x: 4, y: 4 (y_hi: 2, y_lo: 2; y = y_hi * 2 + y_lo), z: 8, core: 2. Of those that a mesh axis runs over, the one named last changes fastest.
Arguments:
- queries: bfloat16 [20, 32768, 128], P(None, ('blk', 'grp')), may hold values from -125 to 125
- keys: bfloat16 [20, 32768, 128], P(None, ('blk', 'grp')), may hold values from -6 to 6
- values: bfloat16 [20, 32768, 128], P(None, ('blk', 'grp')), may hold values from -6 to 6
- tile_cluster: int32 [20, 256], P(None, ('blk', 'grp')), may hold values from 0 to 255, as said below
Outputs:
- attended: bfloat16 [20, 32768, 128], P(None, ('blk', 'grp'))
Inputs may be any that keep to these rules, and one draw needn't show every extreme that they name: `tile_cluster`: cluster c is served by grp index c % 16. In each group of 16 consecutive tiles (one blk index), over all heads, every server has exactly 20 tiles, at most 2 of them at one tile index; the tiles of one head with one cluster in one group are exactly 4 or none. Cluster numbers are uneven: low ones are far more common.
All inputs are finite; a program needn't handle non-finite values.
Results may differ from a plain program's by a relative error of at most 0.0038.
Values may be sent and summed in bfloat16 or wider, within the bound.
No kernel may reach another device: no remote copies, remote signals or barrier semaphores. Data moves between devices by JAX's collectives and lax.ppermute only.
A program may use at most 128 MiB of HBM per device.

v0:
```python
from functools import partial

import jax
import jax.numpy as jnp
from jax import lax
from jax.experimental import pallas as pl
from jax.experimental.pallas import tpu as pltpu
from jax.sharding import Mesh
from jax.sharding import PartitionSpec as P

AXES = ("ylo", "z", "yhi", "x", "core")
PLANE = ("ylo", "yhi", "x", "core")
SIZES = (2, 8, 2, 4, 2)

HEADS = 20
PLANES = 8
PER_PLANE = 3
SLOT_HEADS = PLANES * PER_PLANE
SERVERS = 32
GROUPS = 16
GROUP_TILES = 16
TILES = 256
TILE = 128
MATCH = 4
UNITS = PER_PLANE * GROUPS * GROUP_TILES // MATCH
PIECE = TILE // SERVERS
HEAD_SIZE = 128
CAPACITIES = ((21, 7), (22, 7), (25, 8), (32, 11), (72, 24))
SPLIT = 7
SPLIT_AGAIN = 9
SCALE = 64
STEP = 8
ROWS = MATCH * TILE
UNIT_PIECE = MATCH * PIECE
NEGATIVE = -1e30
VMEM = 56 * 1024 * 1024


def assign_kernel(count_ref, size_ref, key_ref, load_ref):
    lane = lax.broadcasted_iota(jnp.int32, (PLANES, 128), 1)
    lane_number = lane.astype(jnp.float32)
    load_ref[...] = jnp.where(lane < SERVERS, 0.0, 65536.0)

    def step(i, carry):
        load = load_ref[...]
        key = jnp.min(load * 128.0 + lane_number, axis=1, keepdims=True)
        owner = key - jnp.floor(key * (1.0 / 128.0)) * 128.0
        load_ref[...] = load + jnp.where(lane_number == owner, size_ref[i], 0.0)
        key_ref[i] = jnp.broadcast_to(key, (PLANES, 128))
        return carry

    lax.fori_loop(0, count_ref[0], step, 0)


def assign(count, sizes):
    return pl.pallas_call(
        assign_kernel,
        in_specs=[
            pl.BlockSpec(memory_space=pltpu.SMEM),
            pl.BlockSpec(memory_space=pltpu.VMEM),
        ],
        out_specs=[pl.BlockSpec(memory_space=pltpu.VMEM)] * 2,
        out_shape=[
            jax.ShapeDtypeStruct((UNITS, PLANES, 128), jnp.float32),
            jax.ShapeDtypeStruct((PLANES, 128), jnp.float32),
        ],
        compiler_params=pltpu.CompilerParams(vmem_limit_bytes=VMEM),
        name="assign",
    )(count, sizes)


def slab(code, depth, start, width):
    owner = lax.shift_right_logical(code, SCALE.bit_length() - 1)
    return owner * depth + start + (code & (SCALE - 1)) * width


def move_units(steps, tile_ref, move):
    def some(i, carry):
        moves = []
        for k in range(STEP):
            unit = i * STEP + k
            moves += move(unit, [tile_ref[unit * MATCH + j] for j in range(MATCH)])
        pieces = [load() for load, _ in moves]
        for piece, (_, store) in zip(pieces, moves):
            store(piece)
        return carry

    lax.fori_loop(0, steps, some, 0)


def mover(in_ref, source, out_ref, target):
    def store(piece):
        out_ref[target] = piece

    return lambda: in_ref[source], store


def pack_kernel(caps, count_ref, tile_ref, place_ref, in_ref, out_ref):
    depth = caps[0]

    def first(unit, tiles):
        to_query = slab(place_ref[unit], depth, depth - 1, -1) * MATCH
        to_keys = slab(place_ref[UNITS + unit], depth, 0, 2) * MATCH
        return [
            mover(in_ref, tile * 3 + s, out_ref, slot + j)
            for j, tile in enumerate(tiles)
            for s, slot in enumerate((to_query, to_keys, to_keys + MATCH))
        ]

    move_units(lax.shift_right_logical(count_ref[0], STEP.bit_length() - 1), tile_ref, first)

    def again(i, carry):
        entry = place_ref[4 * UNITS + i]
        unit = jnp.where(entry >= UNITS, entry - UNITS, entry)
        also = slab(place_ref[2 * UNITS + entry], depth, 0, 2) * MATCH
        tiles = [tile_ref[unit * MATCH + j] for j in range(MATCH)]
        pieces = [in_ref[tile * 3 + s] for s in (1, 2) for tile in tiles]
        for k, piece in enumerate(pieces):
            out_ref[also + k] = piece
        return carry

    lax.fori_loop(0, count_ref[1], again, 0)


def pack(caps, count, tiles, place, arrived):
    smem = pl.BlockSpec(memory_space=pltpu.SMEM)
    vmem = pl.BlockSpec(memory_space=pltpu.VMEM)
    return pl.pallas_call(
        partial(pack_kernel, caps),
        in_specs=[smem, smem, smem, vmem],
        out_specs=vmem,
        out_shape=jax.ShapeDtypeStruct(
            (SERVERS * caps[0] * MATCH, PIECE, HEAD_SIZE), jnp.bfloat16
        ),
        compiler_params=pltpu.CompilerParams(vmem_limit_bytes=VMEM),
        name="pack_units",
    )(count, tiles, place, arrived)


def unpack_kernel(caps, count_ref, tile_ref, place_ref, in_ref, out_ref):
    out_ref = out_ref.reshape(TILES * PER_PLANE, PIECE, HEAD_SIZE)

    def back(unit, tiles):
        slot = slab(place_ref[unit], caps[1], 0, 1) * MATCH
        return [mover(in_ref, slot + j, out_ref, tile) for j, tile in enumerate(tiles)]

    move_units(lax.shift_right_logical(count_ref[0], STEP.bit_length() - 1), tile_ref, back)


def unpack(caps, count, tiles, place, results):
    smem = pl.BlockSpec(memory_space=pltpu.SMEM)
    vmem = pl.BlockSpec(memory_space=pltpu.VMEM)
    return pl.pallas_call(
        partial(unpack_kernel, caps),
        in_specs=[smem, smem, smem, vmem],
        out_specs=vmem,
        out_shape=jax.ShapeDtypeStruct((TILES, PER_PLANE, PIECE, HEAD_SIZE), jnp.bfloat16),
        compiler_params=pltpu.CompilerParams(vmem_limit_bytes=VMEM),
        name="unpack_units",
    )(count, tiles, place, results)


def spread_kernel(*refs):
    out_ref = refs[3]
    half = SERVERS // 2
    for s in range(3):
        for head in range(HEADS):
            plane, slot = divmod(head, PER_PLANE)
            for y in range(2):
                devices = pl.ds((y * PLANES + plane) * half, half)
                out_ref[devices, slot * 3 + s] = refs[s][head, y * half : (y + 1) * half]


def spread(queries, keys, values):
    vmem = pl.BlockSpec(memory_space=pltpu.VMEM)
    pieces = [a.reshape(HEADS, SERVERS, PIECE, HEAD_SIZE) for a in (queries, keys, values)]
    return pl.pallas_call(
        spread_kernel,
        in_specs=[vmem] * 3,
        out_specs=vmem,
        out_shape=jax.ShapeDtypeStruct((TILES, PER_PLANE * 3, PIECE, HEAD_SIZE), jnp.bfloat16),
        compiler_params=pltpu.CompilerParams(vmem_limit_bytes=VMEM),
        name="spread_rows",
    )(*pieces)


def row_key(shape, dim):
    row = lax.broadcasted_iota(jnp.int32, shape, dim)
    piece = row // UNIT_PIECE
    tile = lax.rem(row // PIECE, MATCH)
    return tile * TILE + piece * PIECE + lax.rem(row, PIECE)


def attend_kernel(
    caps, used_ref, table_ref, in_ref, out_ref, peak_ref, total_ref, sum_ref, turned_ref, *score_refs
):
    factor = HEAD_SIZE**-0.5 * 1.4426950408889634

    def rows(which):
        return in_ref[:, which].reshape(ROWS, HEAD_SIZE)

    def turn(unit, carry):
        turned_ref[unit] = rows(2 * unit + 1).T
        return carry

    lax.fori_loop(0, used_ref[1], turn, 0)

    def one_query_unit(slot, carry):
        code = table_ref[slot]
        first = lax.shift_right_logical(code, SCALE.bit_length() - 1)
        earlier = code & (SCALE - 1)
        last = first + earlier
        query = rows(caps[0] - 1 - slot)

        def scores_of(unit):
            return lax.dot_general(
                rows(2 * unit), query, (((1,), (1,)), ((), ())), preferred_element_type=jnp.float32
            )

        def unit_at(step):
            return jnp.where(step == 0, last, jnp.minimum(first + step - 1, last))

        def fold(step, now):
            score_refs[1 - now][...] = scores_of(unit_at(step + 1))
            scores = score_refs[now][...]
            old = peak_ref[...]
            peak = jnp.maximum(old, jnp.max(scores, axis=0, keepdims=True))
            weights = jnp.exp2((scores - peak) * factor)
            keep = jnp.exp2((old - peak) * factor)
            peak_ref[...] = peak
            total_ref[...] = total_ref[...] * keep + jnp.sum(weights, axis=0, keepdims=True)
            sum_ref[...] = sum_ref[...] * keep + jnp.dot(
                turned_ref[unit_at(step)],
                weights.astype(jnp.bfloat16),
                preferred_element_type=jnp.float32,
            )

        visible = row_key((ROWS, 1), 0) <= row_key((1, ROWS), 1)
        score_refs[0][...] = jnp.where(visible, scores_of(last), NEGATIVE)
        peak_ref[...] = jnp.full(peak_ref.shape, NEGATIVE, jnp.float32)
        total_ref[...] = jnp.zeros(total_ref.shape, jnp.float32)
        sum_ref[...] = jnp.zeros(sum_ref.shape, jnp.float32)

        def two(i, carry):
            fold(2 * i, 0)
            fold(2 * i + 1, 1)
            return carry

        lax.fori_loop(0, lax.shift_right_logical(earlier + 1, 1), two, 0)

        @pl.when((earlier & 1) == 0)
        def _():
            fold(earlier, 0)

        result = (sum_ref[...] / total_ref[...]).T.astype(jnp.bfloat16)
        out_ref[:, slot] = result.reshape(SERVERS, UNIT_PIECE, HEAD_SIZE)
        return carry

    lax.fori_loop(0, used_ref[0], one_query_unit, 0)


def attend(caps, used, table, units):
    smem = pl.BlockSpec(memory_space=pltpu.SMEM)
    vmem = pl.BlockSpec(memory_space=pltpu.VMEM)
    return pl.pallas_call(
        partial(attend_kernel, caps),
        in_specs=[smem, smem, vmem],
        out_specs=vmem,
        out_shape=jax.ShapeDtypeStruct((SERVERS, caps[1], UNIT_PIECE, HEAD_SIZE), jnp.bfloat16),
        scratch_shapes=[
            pltpu.VMEM((1, ROWS), jnp.float32),
            pltpu.VMEM((1, ROWS), jnp.float32),
            pltpu.VMEM((HEAD_SIZE, ROWS), jnp.float32),
            pltpu.VMEM((caps[0] // 2, HEAD_SIZE, ROWS), jnp.bfloat16),
            pltpu.VMEM((ROWS, ROWS), jnp.float32),
            pltpu.VMEM((ROWS, ROWS), jnp.float32),
        ],
        compiler_params=pltpu.CompilerParams(vmem_limit_bytes=VMEM),
        name="attend",
    )(used, table, units)


def plan(clusters):
    plane = lax.axis_index("z")
    server = lax.axis_index(PLANE)
    clusters = jnp.pad(clusters.T, ((0, SLOT_HEADS - HEADS), (0, 0)))
    tiles = clusters.reshape(SLOT_HEADS, GROUPS, GROUP_TILES)
    index = jnp.arange(GROUP_TILES, dtype=jnp.int32)
    mine, other = tiles[:, :, :, None], tiles[:, :, None, :]
    ahead = (other < mine) | ((other == mine) & (index[None, :] < index[:, None]))
    place = jnp.sum(ahead, axis=3, dtype=jnp.int32)
    at_place = place[:, :, None, :] == index[:, None]
    unit_cluster = jnp.sum(
        jnp.where(at_place[:, :, ::MATCH], tiles[:, :, None, :], 0), axis=3
    ).reshape(SLOT_HEADS, -1)
    units = unit_cluster.shape[1]
    number = jnp.arange(units, dtype=jnp.int32)
    same = unit_cluster[:, :, None] == unit_cluster[:, None, :]
    size = jnp.sum(same, axis=2, dtype=jnp.int32)
    rank = jnp.sum(same & (number[None, :] < number[:, None]), axis=2, dtype=jnp.int32)
    real = jnp.arange(SLOT_HEADS)[:, None] < HEADS
    again_cut = size >= SPLIT_AGAIN
    cut = jnp.where(again_cut, size * 6 // 10, jnp.where(size >= SPLIT, size * 7 // 10, 0))
    last_cut = jnp.where(again_cut, size * 8 // 10, cut)
    lead = (rank == 0) & real
    number_of_tasks = 3 * UNITS

    def loads(keys, queries):
        load = (2 * keys + queries) * SCALE + queries
        return jnp.where(lead & (queries > 0), load, 0).reshape(PLANES, UNITS)

    tasks = jnp.concatenate(
        [loads(size, size - last_cut), loads(cut, cut), loads(last_cut, last_cut - cut)], axis=1
    )
    every = jnp.arange(number_of_tasks, dtype=jnp.int32)
    mine, other = tasks[:, :, None], tasks[:, None, :]
    order = jnp.sum(
        (other > mine) | ((other == mine) & (every[None, :] < every[:, None])),
        axis=2,
        dtype=jnp.int32,
    )
    sizes = jnp.sum(
        jnp.where(order[:, None, :] == every[:UNITS, None], tasks[:, None, :], 0), axis=2
    )
    count = jnp.max(jnp.sum(tasks > 0, axis=1, dtype=jnp.int32)).reshape(1)
    sizes = jnp.broadcast_to(
        sizes.T.astype(jnp.float32)[:, :, None], (UNITS, PLANES, 128)
    )
    key, load = assign(count, sizes)
    load = jnp.where(jnp.arange(128)[None, :] < SERVERS, load, 0.0).astype(jnp.int32)
    most = jnp.max(load // SCALE), jnp.max(load % SCALE)
    key = lax.dynamic_slice(key, (0, plane, 0), (UNITS, 1, 1)).reshape(UNITS).astype(jnp.int32)
    load = lax.dynamic_index_in_dim(load, plane, 0, keepdims=False)
    first = plane * PER_PLANE

    def own(array):
        return lax.dynamic_slice_in_dim(array, first, PER_PLANE, 0)

    own_order = lax.dynamic_index_in_dim(order, plane, 0, keepdims=False)
    own_order = own_order.reshape(3, PER_PLANE, 1, units)
    own_rank, own_cut, own_last_cut = own(rank), own(cut), own(last_cut)
    leader = own(same) & (own_rank == 0)[:, None, :]
    task = jnp.sum(jnp.where(leader, own_order, 0), axis=3).reshape(3, UNITS)
    code = jnp.sum(
        jnp.where(task[:, :, None] == every[:UNITS], key, 0), axis=2
    )
    own_rank, own_cut = own_rank.reshape(UNITS), own_cut.reshape(UNITS)
    own_last_cut = own_last_cut.reshape(UNITS)
    owner, before = code % 128, code // 128
    query_base = before % SCALE
    base = (before // SCALE - query_base) // 2
    own_count = jnp.clip(HEADS - first, 0, PER_PLANE) * units
    live = every[:UNITS] < own_count
    in_front = (own_rank < own_cut) & live
    in_second = (own_rank < own_last_cut) & (own_last_cut > own_cut) & live

    def of_task(first, second, last):
        return jnp.where(in_front, first, jnp.where(in_second, second, last))

    query_owner = of_task(owner[1], owner[2], owner[0])
    query_slot = own_rank + of_task(
        query_base[1], query_base[2] - own_cut, query_base[0] - own_last_cut
    )
    copied = jnp.concatenate([in_front, in_second])
    entries = every[: 2 * UNITS]
    earlier = jnp.sum(
        copied[None, :] & (entries[None, :] < entries[:, None]), axis=1, dtype=jnp.int32
    )
    again = jnp.sum(
        jnp.where(copied[None, :] & (earlier[None, :] == entries[:, None]), entries[None, :], 0),
        axis=1,
    )
    place = jnp.concatenate(
        [query_owner * SCALE + query_slot]
        + [owner[i] * SCALE + base[i] + own_rank for i in range(3)]
        + [again]
    )
    tile_of = own(
        jnp.sum(jnp.where(at_place, index, 0), axis=3, dtype=jnp.int32)
    ) + jnp.arange(GROUPS, dtype=jnp.int32)[:, None] * GROUP_TILES
    here = (
        ((query_owner == server) & live)[None, :]
        & (query_slot[None, :] == jnp.arange(SCALE, dtype=jnp.int32)[:, None])
    )
    table = of_task(base[1], base[2], base[0]) * SCALE + own_rank
    table = jnp.sum(jnp.where(here, table[None, :], 0), axis=1)
    mine = jnp.sum(jnp.where(jnp.arange(128) == server, load, 0))
    used = jnp.stack([mine % SCALE, (mine // SCALE - mine % SCALE) // 2])
    counts = jnp.stack([own_count, jnp.sum(copied, dtype=jnp.int32)])
    tile_of = tile_of * PER_PLANE + jnp.arange(PER_PLANE, dtype=jnp.int32)[:, None, None]
    return (counts, tile_of.reshape(-1), place, table, used), most


def exchange(caps, arrived, count, tiles, place, table, used):
    pieces = arrived.reshape(-1, PIECE, HEAD_SIZE)
    packed = pack(caps, count, tiles, place, pieces)
    packed = packed.reshape(SERVERS, -1, UNIT_PIECE, HEAD_SIZE)
    units = lax.all_to_all(packed, PLANE, split_axis=0, concat_axis=0, tiled=True)
    results = attend(caps, used, table, units)
    results = lax.all_to_all(results, PLANE, split_axis=0, concat_axis=0, tiled=True)
    results = results.reshape(SERVERS * caps[1] * MATCH, PIECE, HEAD_SIZE)
    return unpack(caps, count, tiles, place, results)


def on_device(queries, keys, values, tile_cluster):
    clusters = jnp.broadcast_to(tile_cluster.reshape(1, 1, HEADS), (TILES, 1, HEADS))
    clusters = lax.all_to_all(clusters, AXES, split_axis=0, concat_axis=0, tiled=True)
    clusters = clusters.reshape(TILES, HEADS)
    outgoing = spread(queries, keys, values)
    arrived = lax.all_to_all(outgoing, AXES, split_axis=0, concat_axis=0, tiled=True)
    tables, (most_slabs, most_queries) = plan(clusters)
    which = jnp.int32(len(CAPACITIES) - 1)
    for i in range(len(CAPACITIES) - 2, -1, -1):
        fits = (most_slabs <= CAPACITIES[i][0]) & (most_queries <= CAPACITIES[i][1])
        which = jnp.where(fits, i, which)
    back = lax.switch(which, [partial(exchange, caps) for caps in CAPACITIES], arrived, *tables)
    back = lax.all_to_all(back, AXES, split_axis=0, concat_axis=0, tiled=True)
    back = back.reshape(2, PLANES, SERVERS // 2, PER_PLANE, PIECE, HEAD_SIZE)
    back = back.transpose(1, 3, 0, 2, 4, 5).reshape(SLOT_HEADS, TILE, HEAD_SIZE)
    return back[:HEADS]


def solution(mesh):
    fine = Mesh(mesh.devices.reshape(SIZES), AXES)
    rows = ("ylo", "z", "yhi", "x", "core")
    return jax.shard_map(
        on_device,
        mesh=fine,
        in_specs=(
            P(None, rows, None),
            P(None, rows, None),
            P(None, rows, None),
            P(None, rows),
        ),
        out_specs=P(None, rows, None),
        check_vma=False,
    )
```

profile of v0, /device:TPU:1, one launch (start us, length us, event | category | flops | bytes accessed | tf_op | source)
XLA Modules:
  0.0 209.6 jit_solution(8816553001838926936)
XLA Ops:
  0.0 1.4 broadcast_in_dim.148
  1.4 15.7 %all-to-all-start.10 = ((s32[256,1,20]{2,1,0:T(1,128)}), s32[256,1,20]{2,1,0:T(1,128)S(1)}, u32[]{:S(2)}, u32[]{:S(2)}) async-start(s32[256,1,20]{2,1,0:T(1,128)} %broadcast_in_dim.148), calls=%async_computation.10 | async-start | bytes 262144 | tf_op jit(solution)/shard_map/all_to_all | solution.py:407
  17.4 3.6 %spread_rows.1 = bf16[256,9,4,128]{3,2,1,0:T(4,128)(2,1)} custom-call(bf16[20,32,4,128]{3,2,1,0:T(4,128)(2,1)} %bitcast.67, bf16[20,32,4,128]{3,2,1,0:T(4,128)(2,1)} %bitcast.68, bf16[20,32,4,128]{3,2,1,0:T(4,128)(2,1)} %bitcast.69), custom_call_target="tpu_custom_call" | custom-call | tf_op jit(solution)/shard_map/spread_rows/pallas_call | solution.py:177
  21.0 8.7 %all-to-all-done.10 = s32[256,1,20]{2,1,0:T(1,128)S(1)} async-done(((s32[256,1,20]{2,1,0:T(1,128)}), s32[256,1,20]{2,1,0:T(1,128)S(1)}, u32[]{:S(2)}, u32[]{:S(2)}) %all-to-all-start.10) | async-done | bytes 20512 | tf_op jit(solution)/shard_map/all_to_all | solution.py:407
  29.7 6.2 %all-to-all-start.11 = ((bf16[256,9,4,128]{3,2,1,0:T(4,128)(2,1)}), bf16[256,9,4,128]{3,2,1,0:T(4,128)(2,1)S(1)}, u32[]{:S(2)}, u32[]{:S(2)}) async-start(bf16[256,9,4,128]{3,2,1,0:T(4,128)(2,1)} %spread_rows.1), calls=%async_computation.11 | async-start | bytes 4718592 | tf_op jit(solution)/shard_map/all_to_all | solution.py:410
  35.9 0.9 convert_reduce_fusion.1
  36.8 0.3 iota_compare_fusion
  37.3 1.2 convert_reduce_fusion.3
  38.8 4.0 %convert_reduce_fusion = s32[8,576]{1,0:T(8,128)S(1)} fusion(s32[8,576]{1,0:T(8,128)S(1)} %get-tuple-element.123, pred[576,576]{1,0:T(8,128)(4,1)S(1)} %iota_compare_fusion.1), kind=kLoop, calls=%fused_computation | loop fusion | flops 15920640 | bytes 368640 | tf_op jit(solution)/shard_map/reduce_sum | solution.py:317
  42.9 0.6 select_reduce_fusion
  43.6 0.7 reduce_max.27
  44.2 1.1 broadcast_in_dim.153.size_ref
  45.4 12.2 %assign.1 = (f32[192,8,128]{2,1,0:T(8,128)}, f32[8,128]{1,0:T(8,128)}) custom-call(s32[1]{0:T(128)} %bitcast.20.count_ref, f32[192,8,128]{2,1,0:T(8,128)} %broadcast_in_dim.153.size_ref), custom_call_target="tpu_custom_call" | custom-call | tf_op jit(solution)/shard_map/assign/pallas_call | solution.py:56
  57.5 1.4 fusion.15
  59.0 0.6 fusion.26
  62.2 0.6 select_reduce_fusion.1
  63.7 0.3 broadcast_compare_fusion
  69.0 4.6 %convert_reduce_fusion.5 = s32[192]{0:T(256)S(1)} fusion(f32[192,8,128]{2,1,0:T(8,128)} %get-tuple-element.104, s32[]{:T(128)S(6)} %select_n.217), kind=kLoop, calls=%fused_computation.14 | loop fusion | flops 192 | bytes 1540 | tf_op jit(solution)/shard_map/convert_element_type | solution.py:332
  73.6 0.3 select_reduce_fusion.3
  74.0 0.8 convert_reduce_fusion.7
  75.1 0.3 select_reduce_fusion.2
  75.4 0.8 pad_add_fusion.2
  76.3 18.2 %all-to-all-done.11 = bf16[256,9,4,128]{3,2,1,0:T(4,128)(2,1)S(1)} async-done(((bf16[256,9,4,128]{3,2,1,0:T(4,128)(2,1)}), bf16[256,9,4,128]{3,2,1,0:T(4,128)(2,1)S(1)}, u32[]{:S(2)}, u32[]{:S(2)}) %all-to-all-start.11) | async-done | bytes 2359328 | tf_op jit(solution)/shard_map/all_to_all | solution.py:410
  94.5 82.9 %conditional.1 = (bf16[256,3,4,128]{3,2,1,0:T(4,128)(2,1)S(1)}) conditional(s32[]{:T(128)} %clamp.3, (bf16[256,9,4,128]{3,2,1,0:T(4,128)(2,1)S(1)}, s32[2]{0:T(128)S(1)}, s32[768]{0:T(1024)S(1)}, s32[1152]{0:T(1024)S(1)}, s32[2]{0:T(128)S(1)}, /*index=5*/s32[64]{0:T(128)S(1)}) %tuple.20, ...), branch_computations={%region_18.19_spmd, %region_19.20_spmd, %region_20.21_spmd, %regio... | conditional | bytes 25165832 | solution.py:416
  94.5 4.6 %pack_units.5 = bf16[2688,4,128]{2,1,0:T(4,128)(2,1)} custom-call(s32[2]{0:T(128)S(1)} %get-tuple-element.62.count_ref, s32[768]{0:T(1024)S(1)} %get-tuple-element.70.tile_ref, s32[1152]{0:T(1024)S(1)} %get-tuple-element.72.place_ref, bf16[2304,4,128]{2,1,0:T(4,128)(2,1)S(1)} %bitcast.48), custom_call_target="tpu_custom_call" | custom-call | tf_op jit(solution)/shard_map/cond/branch_0_fun/pack_units/pallas_call | solution.py:128
  99.1 41.1 %all_to_all.55.in_ref = bf16[32,21,16,128]{3,2,1,0:T(8,128)(2,1)} all-to-all(bf16[32,21,16,128]{3,2,1,0:T(8,128)(2,1)} %bitcast.58), channel_id=1, replica_groups=mesh['ylo'=2,'z'=8,'yhi'=2,'x'=4,'core'=2] {'ylo','yhi','x','core'}, dimensions={0} | all-to-all | bytes 5505024 | tf_op jit(solution)/shard_map/cond/branch_0_fun/all_to_all | solution.py:398
  140.3 13.7 %attend.5 = bf16[32,7,16,128]{3,2,1,0:T(8,128)(2,1)} custom-call(s32[2]{0:T(128)S(1)} %get-tuple-element.74.used_ref, s32[64]{0:T(128)S(1)} %get-tuple-element.75.table_ref, bf16[32,21,16,128]{3,2,1,0:T(8,128)(2,1)} %all_to_all.55.in_ref), custom_call_target="tpu_custom_call" | custom-call | tf_op jit(solution)/shard_map/cond/branch_0_fun/attend/pallas_call | solution.py:265
  154.0 20.5 %all_to_all.56 = bf16[32,7,16,128]{3,2,1,0:T(8,128)(2,1)} all-to-all(bf16[32,7,16,128]{3,2,1,0:T(8,128)(2,1)} %attend.5), channel_id=1, replica_groups=mesh['ylo'=2,'z'=8,'yhi'=2,'x'=4,'core'=2] {'ylo','yhi','x','core'}, dimensions={0} | all-to-all | bytes 1835008 | tf_op jit(solution)/shard_map/cond/branch_0_fun/all_to_all | solution.py:400
  174.5 2.9 %unpack_units.5 = bf16[256,3,4,128]{3,2,1,0:T(4,128)(2,1)S(1)} custom-call(s32[2]{0:T(128)S(1)} %get-tuple-element.62.count_ref, s32[768]{0:T(1024)S(1)} %get-tuple-element.70.tile_ref, s32[1152]{0:T(1024)S(1)} %get-tuple-element.72.place_ref, bf16[896,4,128]{2,1,0:T(4,128)(2,1)} %bitcast.61), custom_call_target="tpu_custom_call" | custom-call | tf_op jit(solution)/shard_map/cond/branch_0_fun/unpack_units/pallas_call | solution.py:153
  177.4 30.9 %all_to_all.65 = bf16[256,3,4,128]{3,2,1,0:T(4,128)(2,1)S(1)} all-to-all(bf16[256,3,4,128]{3,2,1,0:T(4,128)(2,1)S(1)} %get-tuple-element.150), channel_id=1, replica_groups=mesh['ylo'=2,'z'=8,'yhi'=2,'x'=4,'core'=2] {'ylo','z','yhi','x','core'}, dimensions={0} | all-to-all | bytes 1572864 | tf_op jit(solution)/shard_map/all_to_all | solution.py:417
  208.3 0.4 copy.33
  208.7 0.9 slice.77
  (46 shorter events, 2.8 us)
Async XLA Ops:
  1.4 28.3 %all-to-all-start.10 = ((s32[256,1,20]{2,1,0:T(1,128)}), s32[256,1,20]{2,1,0:T(1,128)S(1)}, u32[]{:S(2)}, u32[]{:S(2)}) async-start(s32[256,1,20]{2,1,0:T(1,128)} %broadcast_in_dim.148), calls=%async_computation.10 | async-start | bytes 262144 | tf_op jit(solution)/shard_map/all_to_all | solution.py:407
  29.7 64.8 %all-to-all-start.11 = ((bf16[256,9,4,128]{3,2,1,0:T(4,128)(2,1)}), bf16[256,9,4,128]{3,2,1,0:T(4,128)(2,1)S(1)}, u32[]{:S(2)}, u32[]{:S(2)}) async-start(bf16[256,9,4,128]{3,2,1,0:T(4,128)(2,1)} %spread_rows.1), calls=%async_computation.11 | async-start | bytes 4718592 | tf_op jit(solution)/shard_map/all_to_all | solution.py:410
where the time goes:
time: 210 us
  blocking collectives  92.5 us (44%)
  Pallas kernels  37 us (18%)
  waiting for transfers between devices  26.9 us (13%)
  starting transfers between devices  21.8 us (10%)
  other arithmetic  18.6 us (9%)
  between operations  7.56 us (4%)
  local copies, waits for them, and re-layouts  5.24 us (2%)
    all_to_all x1, blocking collectives, exchange(): lax.all_to_all(packed, PLANE, split_axis=0, concat_axis=0, tiled=True)  41.1 us
    all_to_all x1, blocking collectives, on_device(): back = lax.all_to_all(back, AXES, split_axis=0, concat_axis=0, tiled=True)  30.9 us
    all_to_all x1, blocking collectives, exchange(): lax.all_to_all(results, PLANE, split_axis=0, concat_axis=0, tiled=True)  20.5 us
    all_to_all x1, waiting for transfers between devices, on_device(): lax.all_to_all(outgoing, AXES, split_axis=0, concat_axis=0, tiled=True)  18.2 us
    all_to_all x1, starting transfers between devices, on_device(): lax.all_to_all(clusters, AXES, split_axis=0, concat_axis=0, tiled=True)  15.7 us
    pallas_call x1, Pallas kernels, attend(): pl.pallas_call(partial(attend_kernel, caps), in_specs=[smem, smem, vmem],...  13.7 us
    pallas_call x1, Pallas kernels, assign(): pl.pallas_call(assign_kernel, in_specs=[pl.BlockSpec(memory_space=pltpu.S...  12.2 us
    all_to_all x1, waiting for transfers between devices, on_device(): lax.all_to_all(clusters, AXES, split_axis=0, concat_axis=0, tiled=True)  8.67 us
  transfers between devices with their start and end apart: 2, of which 2 were waited for; matrix products, arithmetic and copies ran while one was open for 10% of the time, Pallas kernels for 8%

commit v1 on v0

--- a/solution.py
+++ b/solution.py
@@ -25,7 +25,7 @@
 UNITS = PER_PLANE * GROUPS * GROUP_TILES // MATCH
 PIECE = TILE // SERVERS
 HEAD_SIZE = 128
-CAPACITIES = ((21, 7), (22, 7), (25, 8), (32, 11), (72, 24))
+CAPACITIES = ((21, 7), (23, 7), (26, 8), (32, 11), (72, 24))
 SPLIT = 7
 SPLIT_AGAIN = 9
 SCALE = 64
@@ -300,8 +300,8 @@
     rank = jnp.sum(same & (number[None, :] < number[:, None]), axis=2, dtype=jnp.int32)
     real = jnp.arange(SLOT_HEADS)[:, None] < HEADS
     again_cut = size >= SPLIT_AGAIN
-    cut = jnp.where(again_cut, size * 6 // 10, jnp.where(size >= SPLIT, size * 7 // 10, 0))
-    last_cut = jnp.where(again_cut, size * 8 // 10, cut)
+    cut = jnp.where(again_cut, size * 13 // 20, jnp.where(size >= SPLIT, size * 7 // 10, 0))
+    last_cut = jnp.where(again_cut, size - 1, cut)
     lead = (rank == 0) & real
     number_of_tasks = 3 * UNITS
 

time: 210 us -> 211 us (level)
  blocking collectives: 92.5 us -> 94.8 us
    all_to_all x1, blocking collectives: 20.5 us -> 22.8 us  [exchange(): lax.all_to_all(results, PLANE, split_axis=0, concat_axis=0, tiled=True)]
where the time goes in v1:
time: 211 us
  blocking collectives  94.8 us (45%)
  Pallas kernels  35.7 us (17%)
  waiting for transfers between devices  26.8 us (13%)
  starting transfers between devices  21.8 us (10%)
  other arithmetic  18.6 us (9%)
  between operations  7.56 us (4%)
  local copies, waits for them, and re-layouts  5.24 us (2%)
    all_to_all x1, blocking collectives, exchange(): lax.all_to_all(packed, PLANE, split_axis=0, concat_axis=0, tiled=True)  41.1 us
    all_to_all x1, blocking collectives, on_device(): back = lax.all_to_all(back, AXES, split_axis=0, concat_axis=0, tiled=True)  30.9 us
    all_to_all x1, blocking collectives, exchange(): lax.all_to_all(results, PLANE, split_axis=0, concat_axis=0, tiled=True)  22.8 us
    all_to_all x1, waiting for transfers between devices, on_device(): lax.all_to_all(outgoing, AXES, split_axis=0, concat_axis=0, tiled=True)  18.1 us
    all_to_all x1, starting transfers between devices, on_device(): lax.all_to_all(clusters, AXES, split_axis=0, concat_axis=0, tiled=True)  15.7 us
    pallas_call x1, Pallas kernels, attend(): pl.pallas_call(partial(attend_kernel, caps), in_specs=[smem, smem, vmem],...  12.3 us
    pallas_call x1, Pallas kernels, assign(): pl.pallas_call(assign_kernel, in_specs=[pl.BlockSpec(memory_space=pltpu.S...  12.3 us
    all_to_all x1, waiting for transfers between devices, on_device(): lax.all_to_all(clusters, AXES, split_axis=0, concat_axis=0, tiled=True)  8.67 us
  transfers between devices with their start and end apart: 2, of which 2 were waited for; matrix products, arithmetic and copies ran while one was open for 10% of the time, Pallas kernels for 8%

profile of v1, /device:TPU:1, one launch (start us, length us, event | category | flops | bytes accessed | tf_op | source)
XLA Modules:
  0.0 210.6 jit_solution(7662827394422529886)
XLA Ops:
  0.0 1.4 broadcast_in_dim.148
  1.4 15.7 %all-to-all-start.10 = ((s32[256,1,20]{2,1,0:T(1,128)}), s32[256,1,20]{2,1,0:T(1,128)S(1)}, u32[]{:S(2)}, u32[]{:S(2)}) async-start(s32[256,1,20]{2,1,0:T(1,128)} %broadcast_in_dim.148), calls=%async_computation.10 | async-start | bytes 262144 | tf_op jit(solution)/shard_map/all_to_all | solution.py:407
  17.4 3.6 %spread_rows.1 = bf16[256,9,4,128]{3,2,1,0:T(4,128)(2,1)} custom-call(bf16[20,32,4,128]{3,2,1,0:T(4,128)(2,1)} %bitcast.67, bf16[20,32,4,128]{3,2,1,0:T(4,128)(2,1)} %bitcast.68, bf16[20,32,4,128]{3,2,1,0:T(4,128)(2,1)} %bitcast.69), custom_call_target="tpu_custom_call" | custom-call | tf_op jit(solution)/shard_map/spread_rows/pallas_call | solution.py:177
  21.0 8.7 %all-to-all-done.10 = s32[256,1,20]{2,1,0:T(1,128)S(1)} async-done(((s32[256,1,20]{2,1,0:T(1,128)}), s32[256,1,20]{2,1,0:T(1,128)S(1)}, u32[]{:S(2)}, u32[]{:S(2)}) %all-to-all-start.10) | async-done | bytes 20512 | tf_op jit(solution)/shard_map/all_to_all | solution.py:407
  29.7 6.2 %all-to-all-start.11 = ((bf16[256,9,4,128]{3,2,1,0:T(4,128)(2,1)}), bf16[256,9,4,128]{3,2,1,0:T(4,128)(2,1)S(1)}, u32[]{:S(2)}, u32[]{:S(2)}) async-start(bf16[256,9,4,128]{3,2,1,0:T(4,128)(2,1)} %spread_rows.1), calls=%async_computation.11 | async-start | bytes 4718592 | tf_op jit(solution)/shard_map/all_to_all | solution.py:410
  35.9 0.9 convert_reduce_fusion.1
  36.8 0.3 iota_compare_fusion
  37.3 1.2 convert_reduce_fusion.3
  38.8 4.0 %convert_reduce_fusion = s32[8,576]{1,0:T(8,128)S(1)} fusion(s32[8,576]{1,0:T(8,128)S(1)} %get-tuple-element.123, pred[576,576]{1,0:T(8,128)(4,1)S(1)} %iota_compare_fusion.1), kind=kLoop, calls=%fused_computation | loop fusion | flops 15920640 | bytes 368640 | tf_op jit(solution)/shard_map/reduce_sum | solution.py:317
  42.9 0.6 select_reduce_fusion
  43.6 0.7 reduce_max.27
  44.2 1.1 broadcast_in_dim.153.size_ref
  45.4 12.3 %assign.1 = (f32[192,8,128]{2,1,0:T(8,128)}, f32[8,128]{1,0:T(8,128)}) custom-call(s32[1]{0:T(128)} %bitcast.20.count_ref, f32[192,8,128]{2,1,0:T(8,128)} %broadcast_in_dim.153.size_ref), custom_call_target="tpu_custom_call" | custom-call | tf_op jit(solution)/shard_map/assign/pallas_call | solution.py:56
  57.6 1.4 fusion.14
  59.0 0.6 fusion.24
  62.3 0.6 select_reduce_fusion.1
  63.8 0.3 broadcast_compare_fusion
  69.1 4.6 %convert_reduce_fusion.5 = s32[192]{0:T(256)S(1)} fusion(f32[192,8,128]{2,1,0:T(8,128)} %get-tuple-element.104, s32[]{:T(128)S(6)} %select_n.208), kind=kLoop, calls=%fused_computation.14 | loop fusion | flops 192 | bytes 1540 | tf_op jit(solution)/shard_map/convert_element_type | solution.py:332
  73.7 0.3 select_reduce_fusion.3
  74.1 0.8 convert_reduce_fusion.7
  75.1 0.3 select_reduce_fusion.2
  75.5 0.8 pad_add_fusion.2
  76.4 18.1 %all-to-all-done.11 = bf16[256,9,4,128]{3,2,1,0:T(4,128)(2,1)S(1)} async-done(((bf16[256,9,4,128]{3,2,1,0:T(4,128)(2,1)}), bf16[256,9,4,128]{3,2,1,0:T(4,128)(2,1)S(1)}, u32[]{:S(2)}, u32[]{:S(2)}) %all-to-all-start.11) | async-done | bytes 2359328 | tf_op jit(solution)/shard_map/all_to_all | solution.py:410
  94.5 83.9 %conditional.1 = (bf16[256,3,4,128]{3,2,1,0:T(4,128)(2,1)S(1)}) conditional(s32[]{:T(128)} %clamp.3, (bf16[256,9,4,128]{3,2,1,0:T(4,128)(2,1)S(1)}, s32[2]{0:T(128)S(1)}, s32[768]{0:T(1024)S(1)}, s32[1152]{0:T(1024)S(1)}, s32[2]{0:T(128)S(1)}, /*index=5*/s32[64]{0:T(128)S(1)}) %tuple.20, ...), branch_computations={%region_18.19_spmd, %region_19.20_spmd, %region_20.21_spmd, %regio... | conditional | bytes 25165832 | solution.py:416
  94.5 4.7 %pack_units.5 = bf16[2688,4,128]{2,1,0:T(4,128)(2,1)} custom-call(s32[2]{0:T(128)S(1)} %get-tuple-element.62.count_ref, s32[768]{0:T(1024)S(1)} %get-tuple-element.70.tile_ref, s32[1152]{0:T(1024)S(1)} %get-tuple-element.72.place_ref, bf16[2304,4,128]{2,1,0:T(4,128)(2,1)S(1)} %bitcast.48), custom_call_target="tpu_custom_call" | custom-call | tf_op jit(solution)/shard_map/cond/branch_0_fun/pack_units/pallas_call | solution.py:128
  99.2 41.1 %all_to_all.55.in_ref = bf16[32,21,16,128]{3,2,1,0:T(8,128)(2,1)} all-to-all(bf16[32,21,16,128]{3,2,1,0:T(8,128)(2,1)} %bitcast.58), channel_id=1, replica_groups=mesh['ylo'=2,'z'=8,'yhi'=2,'x'=4,'core'=2] {'ylo','yhi','x','core'}, dimensions={0} | all-to-all | bytes 5505024 | tf_op jit(solution)/shard_map/cond/branch_0_fun/all_to_all | solution.py:398
  140.3 12.3 %attend.5 = bf16[32,7,16,128]{3,2,1,0:T(8,128)(2,1)} custom-call(s32[2]{0:T(128)S(1)} %get-tuple-element.74.used_ref, s32[64]{0:T(128)S(1)} %get-tuple-element.75.table_ref, bf16[32,21,16,128]{3,2,1,0:T(8,128)(2,1)} %all_to_all.55.in_ref), custom_call_target="tpu_custom_call" | custom-call | tf_op jit(solution)/shard_map/cond/branch_0_fun/attend/pallas_call | solution.py:265
  152.7 22.8 %all_to_all.56 = bf16[32,7,16,128]{3,2,1,0:T(8,128)(2,1)} all-to-all(bf16[32,7,16,128]{3,2,1,0:T(8,128)(2,1)} %attend.5), channel_id=1, replica_groups=mesh['ylo'=2,'z'=8,'yhi'=2,'x'=4,'core'=2] {'ylo','yhi','x','core'}, dimensions={0} | all-to-all | bytes 1835008 | tf_op jit(solution)/shard_map/cond/branch_0_fun/all_to_all | solution.py:400
  175.5 2.9 %unpack_units.5 = bf16[256,3,4,128]{3,2,1,0:T(4,128)(2,1)S(1)} custom-call(s32[2]{0:T(128)S(1)} %get-tuple-element.62.count_ref, s32[768]{0:T(1024)S(1)} %get-tuple-element.70.tile_ref, s32[1152]{0:T(1024)S(1)} %get-tuple-element.72.place_ref, bf16[896,4,128]{2,1,0:T(4,128)(2,1)} %bitcast.61), custom_call_target="tpu_custom_call" | custom-call | tf_op jit(solution)/shard_map/cond/branch_0_fun/unpack_units/pallas_call | solution.py:153
  178.4 30.9 %all_to_all.65 = bf16[256,3,4,128]{3,2,1,0:T(4,128)(2,1)S(1)} all-to-all(bf16[256,3,4,128]{3,2,1,0:T(4,128)(2,1)S(1)} %get-tuple-element.150), channel_id=1, replica_groups=mesh['ylo'=2,'z'=8,'yhi'=2,'x'=4,'core'=2] {'ylo','z','yhi','x','core'}, dimensions={0} | all-to-all | bytes 1572864 | tf_op jit(solution)/shard_map/all_to_all | solution.py:417
  209.3 0.4 copy.33
  209.7 0.9 slice.77
  (46 shorter events, 2.8 us)
Async XLA Ops:
  1.4 28.3 %all-to-all-start.10 = ((s32[256,1,20]{2,1,0:T(1,128)}), s32[256,1,20]{2,1,0:T(1,128)S(1)}, u32[]{:S(2)}, u32[]{:S(2)}) async-start(s32[256,1,20]{2,1,0:T(1,128)} %broadcast_in_dim.148), calls=%async_computation.10 | async-start | bytes 262144 | tf_op jit(solution)/shard_map/all_to_all | solution.py:407
  29.7 64.8 %all-to-all-start.11 = ((bf16[256,9,4,128]{3,2,1,0:T(4,128)(2,1)}), bf16[256,9,4,128]{3,2,1,0:T(4,128)(2,1)S(1)}, u32[]{:S(2)}, u32[]{:S(2)}) async-start(bf16[256,9,4,128]{3,2,1,0:T(4,128)(2,1)} %spread_rows.1), calls=%async_computation.11 | async-start | bytes 4718592 | tf_op jit(solution)/shard_map/all_to_all | solution.py:410

commit v2 on v1

--- a/solution.py
+++ b/solution.py
@@ -220,8 +220,9 @@
         def unit_at(step):
             return jnp.where(step == 0, last, jnp.minimum(first + step - 1, last))
 
-        def fold(step, now):
-            score_refs[1 - now][...] = scores_of(unit_at(step + 1))
+        def fold(step, now, ahead=True):
+            if ahead:
+                score_refs[1 - now][...] = scores_of(unit_at(step + 1))
             scores = score_refs[now][...]
             old = peak_ref[...]
             peak = jnp.maximum(old, jnp.max(scores, axis=0, keepdims=True))
@@ -250,7 +251,7 @@
 
         @pl.when((earlier & 1) == 0)
         def _():
-            fold(earlier, 0)
+            fold(earlier, 0, ahead=False)
 
         result = (sum_ref[...] / total_ref[...]).T.astype(jnp.bfloat16)
         out_ref[:, slot] = result.reshape(SERVERS, UNIT_PIECE, HEAD_SIZE)

time: 211 us -> 212 us (level)
  Pallas kernels: 35.7 us -> 39.4 us
  blocking collectives: 94.8 us -> 91.6 us
    all_to_all x1, blocking collectives: 22.8 us -> 18.4 us  [exchange(): lax.all_to_all(results, PLANE, split_axis=0, concat_axis=0, tiled=True)]
    pallas_call x1, Pallas kernels: 12.3 us -> 15.4 us  [attend(): pl.pallas_call(partial(attend_kernel, caps), in_specs=[smem, smem, vmem],...]
where the time goes in v2:
time: 212 us; the launch traced here: 210 us
  blocking collectives  91.6 us (43%)
  Pallas kernels  39.4 us (19%)
  waiting for transfers between devices  26.2 us (12%)
  starting transfers between devices  21.8 us (10%)
  other arithmetic  18.6 us (9%)
  between operations  7.56 us (4%)
  local copies, waits for them, and re-layouts  5.24 us (2%)
    all_to_all x1, blocking collectives, exchange(): lax.all_to_all(packed, PLANE, split_axis=0, concat_axis=0, tiled=True)  41.1 us
    all_to_all x1, blocking collectives, on_device(): back = lax.all_to_all(back, AXES, split_axis=0, concat_axis=0, tiled=True)  32 us
    all_to_all x1, blocking collectives, exchange(): lax.all_to_all(results, PLANE, split_axis=0, concat_axis=0, tiled=True)  18.4 us
    all_to_all x1, waiting for transfers between devices, on_device(): lax.all_to_all(outgoing, AXES, split_axis=0, concat_axis=0, tiled=True)  17.6 us
    all_to_all x1, starting transfers between devices, on_device(): lax.all_to_all(clusters, AXES, split_axis=0, concat_axis=0, tiled=True)  15.7 us
    pallas_call x1, Pallas kernels, attend(): pl.pallas_call(partial(attend_kernel, caps), in_specs=[smem, smem, vmem],...  15.4 us
    pallas_call x1, Pallas kernels, assign(): pl.pallas_call(assign_kernel, in_specs=[pl.BlockSpec(memory_space=pltpu.S...  12.8 us
    all_to_all x1, waiting for transfers between devices, on_device(): lax.all_to_all(clusters, AXES, split_axis=0, concat_axis=0, tiled=True)  8.67 us
  transfers between devices with their start and end apart: 2, of which 2 were waited for; matrix products, arithmetic and copies ran while one was open for 10% of the time, Pallas kernels for 8%

profile of v2, /device:TPU:1, one launch (start us, length us, event | category | flops | bytes accessed | tf_op | source)
XLA Modules:
  0.0 210.5 jit_solution(5106884680718187544)
XLA Ops:
  0.0 1.4 broadcast_in_dim.148
  1.4 15.7 %all-to-all-start.10 = ((s32[256,1,20]{2,1,0:T(1,128)}), s32[256,1,20]{2,1,0:T(1,128)S(1)}, u32[]{:S(2)}, u32[]{:S(2)}) async-start(s32[256,1,20]{2,1,0:T(1,128)} %broadcast_in_dim.148), calls=%async_computation.10 | async-start | bytes 262144 | tf_op jit(solution)/shard_map/all_to_all | solution.py:408
  17.4 3.6 %spread_rows.1 = bf16[256,9,4,128]{3,2,1,0:T(4,128)(2,1)} custom-call(bf16[20,32,4,128]{3,2,1,0:T(4,128)(2,1)} %bitcast.67, bf16[20,32,4,128]{3,2,1,0:T(4,128)(2,1)} %bitcast.68, bf16[20,32,4,128]{3,2,1,0:T(4,128)(2,1)} %bitcast.69), custom_call_target="tpu_custom_call" | custom-call | tf_op jit(solution)/shard_map/spread_rows/pallas_call | solution.py:177
  21.0 8.7 %all-to-all-done.10 = s32[256,1,20]{2,1,0:T(1,128)S(1)} async-done(((s32[256,1,20]{2,1,0:T(1,128)}), s32[256,1,20]{2,1,0:T(1,128)S(1)}, u32[]{:S(2)}, u32[]{:S(2)}) %all-to-all-start.10) | async-done | bytes 20512 | tf_op jit(solution)/shard_map/all_to_all | solution.py:408
  29.7 6.2 %all-to-all-start.11 = ((bf16[256,9,4,128]{3,2,1,0:T(4,128)(2,1)}), bf16[256,9,4,128]{3,2,1,0:T(4,128)(2,1)S(1)}, u32[]{:S(2)}, u32[]{:S(2)}) async-start(bf16[256,9,4,128]{3,2,1,0:T(4,128)(2,1)} %spread_rows.1), calls=%async_computation.11 | async-start | bytes 4718592 | tf_op jit(solution)/shard_map/all_to_all | solution.py:411
  35.9 0.9 convert_reduce_fusion.1
  36.8 0.3 iota_compare_fusion
  37.3 1.2 convert_reduce_fusion.3
  38.8 4.0 %convert_reduce_fusion = s32[8,576]{1,0:T(8,128)S(1)} fusion(s32[8,576]{1,0:T(8,128)S(1)} %get-tuple-element.123, pred[576,576]{1,0:T(8,128)(4,1)S(1)} %iota_compare_fusion.1), kind=kLoop, calls=%fused_computation | loop fusion | flops 15920640 | bytes 368640 | tf_op jit(solution)/shard_map/reduce_sum | solution.py:318
  42.9 0.6 select_reduce_fusion
  43.6 0.7 reduce_max.27
  44.2 1.1 broadcast_in_dim.153.size_ref
  45.4 12.8 %assign.1 = (f32[192,8,128]{2,1,0:T(8,128)}, f32[8,128]{1,0:T(8,128)}) custom-call(s32[1]{0:T(128)} %bitcast.20.count_ref, f32[192,8,128]{2,1,0:T(8,128)} %broadcast_in_dim.153.size_ref), custom_call_target="tpu_custom_call" | custom-call | tf_op jit(solution)/shard_map/assign/pallas_call | solution.py:56
  58.2 1.4 fusion.14
  59.6 0.6 fusion.24
  62.8 0.6 select_reduce_fusion.1
  64.3 0.3 broadcast_compare_fusion
  69.6 4.6 %convert_reduce_fusion.5 = s32[192]{0:T(256)S(1)} fusion(f32[192,8,128]{2,1,0:T(8,128)} %get-tuple-element.104, s32[]{:T(128)S(6)} %select_n.208), kind=kLoop, calls=%fused_computation.14 | loop fusion | flops 192 | bytes 1540 | tf_op jit(solution)/shard_map/convert_element_type | solution.py:333
  74.3 0.3 select_reduce_fusion.3
  74.7 0.8 convert_reduce_fusion.7
  75.7 0.3 select_reduce_fusion.2
  76.1 0.8 pad_add_fusion.2
  76.9 17.6 %all-to-all-done.11 = bf16[256,9,4,128]{3,2,1,0:T(4,128)(2,1)S(1)} async-done(((bf16[256,9,4,128]{3,2,1,0:T(4,128)(2,1)}), bf16[256,9,4,128]{3,2,1,0:T(4,128)(2,1)S(1)}, u32[]{:S(2)}, u32[]{:S(2)}) %all-to-all-start.11) | async-done | bytes 2359328 | tf_op jit(solution)/shard_map/all_to_all | solution.py:411
  94.5 82.6 %conditional.1 = (bf16[256,3,4,128]{3,2,1,0:T(4,128)(2,1)S(1)}) conditional(s32[]{:T(128)} %clamp.3, (bf16[256,9,4,128]{3,2,1,0:T(4,128)(2,1)S(1)}, s32[2]{0:T(128)S(1)}, s32[768]{0:T(1024)S(1)}, s32[1152]{0:T(1024)S(1)}, s32[2]{0:T(128)S(1)}, /*index=5*/s32[64]{0:T(128)S(1)}) %tuple.20, ...), branch_computations={%region_18.19_spmd, %region_19.20_spmd, %region_20.21_spmd, %regio... | conditional | bytes 25165832 | solution.py:417
  94.5 4.7 %pack_units.5 = bf16[2688,4,128]{2,1,0:T(4,128)(2,1)} custom-call(s32[2]{0:T(128)S(1)} %get-tuple-element.62.count_ref, s32[768]{0:T(1024)S(1)} %get-tuple-element.70.tile_ref, s32[1152]{0:T(1024)S(1)} %get-tuple-element.72.place_ref, bf16[2304,4,128]{2,1,0:T(4,128)(2,1)S(1)} %bitcast.48), custom_call_target="tpu_custom_call" | custom-call | tf_op jit(solution)/shard_map/cond/branch_0_fun/pack_units/pallas_call | solution.py:128
  99.2 41.1 %all_to_all.55.in_ref = bf16[32,21,16,128]{3,2,1,0:T(8,128)(2,1)} all-to-all(bf16[32,21,16,128]{3,2,1,0:T(8,128)(2,1)} %bitcast.58), channel_id=1, replica_groups=mesh['ylo'=2,'z'=8,'yhi'=2,'x'=4,'core'=2] {'ylo','yhi','x','core'}, dimensions={0} | all-to-all | bytes 5505024 | tf_op jit(solution)/shard_map/cond/branch_0_fun/all_to_all | solution.py:399
  140.4 15.4 %attend.5 = bf16[32,7,16,128]{3,2,1,0:T(8,128)(2,1)} custom-call(s32[2]{0:T(128)S(1)} %get-tuple-element.74.used_ref, s32[64]{0:T(128)S(1)} %get-tuple-element.75.table_ref, bf16[32,21,16,128]{3,2,1,0:T(8,128)(2,1)} %all_to_all.55.in_ref), custom_call_target="tpu_custom_call" | custom-call | tf_op jit(solution)/shard_map/cond/branch_0_fun/attend/pallas_call | solution.py:266
  155.8 18.4 %all_to_all.56 = bf16[32,7,16,128]{3,2,1,0:T(8,128)(2,1)} all-to-all(bf16[32,7,16,128]{3,2,1,0:T(8,128)(2,1)} %attend.5), channel_id=1, replica_groups=mesh['ylo'=2,'z'=8,'yhi'=2,'x'=4,'core'=2] {'ylo','yhi','x','core'}, dimensions={0} | all-to-all | bytes 1835008 | tf_op jit(solution)/shard_map/cond/branch_0_fun/all_to_all | solution.py:401
  174.3 2.9 %unpack_units.5 = bf16[256,3,4,128]{3,2,1,0:T(4,128)(2,1)S(1)} custom-call(s32[2]{0:T(128)S(1)} %get-tuple-element.62.count_ref, s32[768]{0:T(1024)S(1)} %get-tuple-element.70.tile_ref, s32[1152]{0:T(1024)S(1)} %get-tuple-element.72.place_ref, bf16[896,4,128]{2,1,0:T(4,128)(2,1)} %bitcast.61), custom_call_target="tpu_custom_call" | custom-call | tf_op jit(solution)/shard_map/cond/branch_0_fun/unpack_units/pallas_call | solution.py:153
  177.2 32.0 %all_to_all.65 = bf16[256,3,4,128]{3,2,1,0:T(4,128)(2,1)S(1)} all-to-all(bf16[256,3,4,128]{3,2,1,0:T(4,128)(2,1)S(1)} %get-tuple-element.150), channel_id=1, replica_groups=mesh['ylo'=2,'z'=8,'yhi'=2,'x'=4,'core'=2] {'ylo','z','yhi','x','core'}, dimensions={0} | all-to-all | bytes 1572864 | tf_op jit(solution)/shard_map/all_to_all | solution.py:418
  209.2 0.4 copy.33
  209.6 0.9 slice.77
  (46 shorter events, 2.8 us)
Async XLA Ops:
  1.4 28.3 %all-to-all-start.10 = ((s32[256,1,20]{2,1,0:T(1,128)}), s32[256,1,20]{2,1,0:T(1,128)S(1)}, u32[]{:S(2)}, u32[]{:S(2)}) async-start(s32[256,1,20]{2,1,0:T(1,128)} %broadcast_in_dim.148), calls=%async_computation.10 | async-start | bytes 262144 | tf_op jit(solution)/shard_map/all_to_all | solution.py:408
  29.7 64.8 %all-to-all-start.11 = ((bf16[256,9,4,128]{3,2,1,0:T(4,128)(2,1)}), bf16[256,9,4,128]{3,2,1,0:T(4,128)(2,1)S(1)}, u32[]{:S(2)}, u32[]{:S(2)}) async-start(bf16[256,9,4,128]{3,2,1,0:T(4,128)(2,1)} %spread_rows.1), calls=%async_computation.11 | async-start | bytes 4718592 | tf_op jit(solution)/shard_map/all_to_all | solution.py:411

commit v3 on v1

--- a/solution.py
+++ b/solution.py
@@ -29,7 +29,7 @@
 SPLIT = 7
 SPLIT_AGAIN = 9
 SCALE = 64
-STEP = 8
+STEP = 16
 ROWS = MATCH * TILE
 UNIT_PIECE = MATCH * PIECE
 NEGATIVE = -1e30

time: 211 us -> 210 us (level)
    all_to_all x1, blocking collectives: 22.8 us -> 20.7 us  [exchange(): lax.all_to_all(results, PLANE, split_axis=0, concat_axis=0, tiled=True)]
  transfers between devices with their start and end apart: 2 -> 2, of which waited for: 2 -> 2; matrix products, arithmetic and copies ran while one was open for 10% -> 10% of each run, Pallas kernels for 8% -> 7%
where the time goes in v3:
time: 210 us; the launch traced here: 209 us
  blocking collectives  93.1 us (44%)
  Pallas kernels  35.8 us (17%)
  waiting for transfers between devices  27 us (13%)
  starting transfers between devices  21.8 us (10%)
  other arithmetic  18.6 us (9%)
  between operations  7.56 us (4%)
  local copies, waits for them, and re-layouts  5.24 us (2%)
    all_to_all x1, blocking collectives, exchange(): lax.all_to_all(packed, PLANE, split_axis=0, concat_axis=0, tiled=True)  41.1 us
    all_to_all x1, blocking collectives, on_device(): back = lax.all_to_all(back, AXES, split_axis=0, concat_axis=0, tiled=True)  31.4 us
    all_to_all x1, blocking collectives, exchange(): lax.all_to_all(results, PLANE, split_axis=0, concat_axis=0, tiled=True)  20.7 us
    all_to_all x1, waiting for transfers between devices, on_device(): lax.all_to_all(outgoing, AXES, split_axis=0, concat_axis=0, tiled=True)  18.4 us
    all_to_all x1, starting transfers between devices, on_device(): lax.all_to_all(clusters, AXES, split_axis=0, concat_axis=0, tiled=True)  15.7 us
    pallas_call x1, Pallas kernels, attend(): pl.pallas_call(partial(attend_kernel, caps), in_specs=[smem, smem, vmem],...  12.3 us
    pallas_call x1, Pallas kernels, assign(): pl.pallas_call(assign_kernel, in_specs=[pl.BlockSpec(memory_space=pltpu.S...  12 us
    all_to_all x1, waiting for transfers between devices, on_device(): lax.all_to_all(clusters, AXES, split_axis=0, concat_axis=0, tiled=True)  8.67 us
  transfers between devices with their start and end apart: 2, of which 2 were waited for; matrix products, arithmetic and copies ran while one was open for 10% of the time, Pallas kernels for 7%

profile of v3, /device:TPU:1, one launch (start us, length us, event | category | flops | bytes accessed | tf_op | source)
XLA Modules:
  0.0 209.3 jit_solution(8672867993837898582)
XLA Ops:
  0.0 1.4 broadcast_in_dim.148
  1.4 15.7 %all-to-all-start.10 = ((s32[256,1,20]{2,1,0:T(1,128)}), s32[256,1,20]{2,1,0:T(1,128)S(1)}, u32[]{:S(2)}, u32[]{:S(2)}) async-start(s32[256,1,20]{2,1,0:T(1,128)} %broadcast_in_dim.148), calls=%async_computation.10 | async-start | bytes 262144 | tf_op jit(solution)/shard_map/all_to_all | solution.py:407
  17.4 3.6 %spread_rows.1 = bf16[256,9,4,128]{3,2,1,0:T(4,128)(2,1)} custom-call(bf16[20,32,4,128]{3,2,1,0:T(4,128)(2,1)} %bitcast.67, bf16[20,32,4,128]{3,2,1,0:T(4,128)(2,1)} %bitcast.68, bf16[20,32,4,128]{3,2,1,0:T(4,128)(2,1)} %bitcast.69), custom_call_target="tpu_custom_call" | custom-call | tf_op jit(solution)/shard_map/spread_rows/pallas_call | solution.py:177
  21.0 8.7 %all-to-all-done.10 = s32[256,1,20]{2,1,0:T(1,128)S(1)} async-done(((s32[256,1,20]{2,1,0:T(1,128)}), s32[256,1,20]{2,1,0:T(1,128)S(1)}, u32[]{:S(2)}, u32[]{:S(2)}) %all-to-all-start.10) | async-done | bytes 20512 | tf_op jit(solution)/shard_map/all_to_all | solution.py:407
  29.7 6.2 %all-to-all-start.11 = ((bf16[256,9,4,128]{3,2,1,0:T(4,128)(2,1)}), bf16[256,9,4,128]{3,2,1,0:T(4,128)(2,1)S(1)}, u32[]{:S(2)}, u32[]{:S(2)}) async-start(bf16[256,9,4,128]{3,2,1,0:T(4,128)(2,1)} %spread_rows.1), calls=%async_computation.11 | async-start | bytes 4718592 | tf_op jit(solution)/shard_map/all_to_all | solution.py:410
  35.9 0.9 convert_reduce_fusion.1
  36.8 0.3 iota_compare_fusion
  37.3 1.2 convert_reduce_fusion.3
  38.8 4.0 %convert_reduce_fusion = s32[8,576]{1,0:T(8,128)S(1)} fusion(s32[8,576]{1,0:T(8,128)S(1)} %get-tuple-element.123, pred[576,576]{1,0:T(8,128)(4,1)S(1)} %iota_compare_fusion.1), kind=kLoop, calls=%fused_computation | loop fusion | flops 15920640 | bytes 368640 | tf_op jit(solution)/shard_map/reduce_sum | solution.py:317
  42.9 0.6 select_reduce_fusion
  43.6 0.7 reduce_max.27
  44.2 1.1 broadcast_in_dim.153.size_ref
  45.4 12.0 %assign.1 = (f32[192,8,128]{2,1,0:T(8,128)}, f32[8,128]{1,0:T(8,128)}) custom-call(s32[1]{0:T(128)} %bitcast.20.count_ref, f32[192,8,128]{2,1,0:T(8,128)} %broadcast_in_dim.153.size_ref), custom_call_target="tpu_custom_call" | custom-call | tf_op jit(solution)/shard_map/assign/pallas_call | solution.py:56
  57.4 1.4 fusion.14
  58.8 0.6 fusion.24
  62.0 0.6 select_reduce_fusion.1
  63.5 0.3 broadcast_compare_fusion
  68.8 4.6 %convert_reduce_fusion.5 = s32[192]{0:T(256)S(1)} fusion(f32[192,8,128]{2,1,0:T(8,128)} %get-tuple-element.104, s32[]{:T(128)S(6)} %select_n.208), kind=kLoop, calls=%fused_computation.14 | loop fusion | flops 192 | bytes 1540 | tf_op jit(solution)/shard_map/convert_element_type | solution.py:332
  73.5 0.3 select_reduce_fusion.3
  73.9 0.8 convert_reduce_fusion.7
  74.9 0.3 select_reduce_fusion.2
  75.3 0.8 pad_add_fusion.2
  76.1 18.4 %all-to-all-done.11 = bf16[256,9,4,128]{3,2,1,0:T(4,128)(2,1)S(1)} async-done(((bf16[256,9,4,128]{3,2,1,0:T(4,128)(2,1)}), bf16[256,9,4,128]{3,2,1,0:T(4,128)(2,1)S(1)}, u32[]{:S(2)}, u32[]{:S(2)}) %all-to-all-start.11) | async-done | bytes 2359328 | tf_op jit(solution)/shard_map/all_to_all | solution.py:410
  94.5 82.1 %conditional.1 = (bf16[256,3,4,128]{3,2,1,0:T(4,128)(2,1)S(1)}) conditional(s32[]{:T(128)} %clamp.3, (bf16[256,9,4,128]{3,2,1,0:T(4,128)(2,1)S(1)}, s32[2]{0:T(128)S(1)}, s32[768]{0:T(1024)S(1)}, s32[1152]{0:T(1024)S(1)}, s32[2]{0:T(128)S(1)}, /*index=5*/s32[64]{0:T(128)S(1)}) %tuple.20, ...), branch_computations={%region_18.19_spmd, %region_19.20_spmd, %region_20.21_spmd, %regio... | conditional | bytes 25165832 | solution.py:416
  94.5 5.1 %pack_units.5 = bf16[2688,4,128]{2,1,0:T(4,128)(2,1)} custom-call(s32[2]{0:T(128)S(1)} %get-tuple-element.62.count_ref, s32[768]{0:T(1024)S(1)} %get-tuple-element.70.tile_ref, s32[1152]{0:T(1024)S(1)} %get-tuple-element.72.place_ref, bf16[2304,4,128]{2,1,0:T(4,128)(2,1)S(1)} %bitcast.48), custom_call_target="tpu_custom_call" | custom-call | tf_op jit(solution)/shard_map/cond/branch_0_fun/pack_units/pallas_call | solution.py:128
  99.6 41.1 %all_to_all.55.in_ref = bf16[32,21,16,128]{3,2,1,0:T(8,128)(2,1)} all-to-all(bf16[32,21,16,128]{3,2,1,0:T(8,128)(2,1)} %bitcast.58), channel_id=1, replica_groups=mesh['ylo'=2,'z'=8,'yhi'=2,'x'=4,'core'=2] {'ylo','yhi','x','core'}, dimensions={0} | all-to-all | bytes 5505024 | tf_op jit(solution)/shard_map/cond/branch_0_fun/all_to_all | solution.py:398
  140.7 12.3 %attend.5 = bf16[32,7,16,128]{3,2,1,0:T(8,128)(2,1)} custom-call(s32[2]{0:T(128)S(1)} %get-tuple-element.74.used_ref, s32[64]{0:T(128)S(1)} %get-tuple-element.75.table_ref, bf16[32,21,16,128]{3,2,1,0:T(8,128)(2,1)} %all_to_all.55.in_ref), custom_call_target="tpu_custom_call" | custom-call | tf_op jit(solution)/shard_map/cond/branch_0_fun/attend/pallas_call | solution.py:265
  153.1 20.7 %all_to_all.56 = bf16[32,7,16,128]{3,2,1,0:T(8,128)(2,1)} all-to-all(bf16[32,7,16,128]{3,2,1,0:T(8,128)(2,1)} %attend.5), channel_id=1, replica_groups=mesh['ylo'=2,'z'=8,'yhi'=2,'x'=4,'core'=2] {'ylo','yhi','x','core'}, dimensions={0} | all-to-all | bytes 1835008 | tf_op jit(solution)/shard_map/cond/branch_0_fun/all_to_all | solution.py:400
  173.7 2.9 %unpack_units.5 = bf16[256,3,4,128]{3,2,1,0:T(4,128)(2,1)S(1)} custom-call(s32[2]{0:T(128)S(1)} %get-tuple-element.62.count_ref, s32[768]{0:T(1024)S(1)} %get-tuple-element.70.tile_ref, s32[1152]{0:T(1024)S(1)} %get-tuple-element.72.place_ref, bf16[896,4,128]{2,1,0:T(4,128)(2,1)} %bitcast.61), custom_call_target="tpu_custom_call" | custom-call | tf_op jit(solution)/shard_map/cond/branch_0_fun/unpack_units/pallas_call | solution.py:153
  176.6 31.4 %all_to_all.65 = bf16[256,3,4,128]{3,2,1,0:T(4,128)(2,1)S(1)} all-to-all(bf16[256,3,4,128]{3,2,1,0:T(4,128)(2,1)S(1)} %get-tuple-element.150), channel_id=1, replica_groups=mesh['ylo'=2,'z'=8,'yhi'=2,'x'=4,'core'=2] {'ylo','z','yhi','x','core'}, dimensions={0} | all-to-all | bytes 1572864 | tf_op jit(solution)/shard_map/all_to_all | solution.py:417
  208.0 0.4 copy.33
  208.4 0.9 slice.77
  (46 shorter events, 2.8 us)
Async XLA Ops:
  1.4 28.3 %all-to-all-start.10 = ((s32[256,1,20]{2,1,0:T(1,128)}), s32[256,1,20]{2,1,0:T(1,128)S(1)}, u32[]{:S(2)}, u32[]{:S(2)}) async-start(s32[256,1,20]{2,1,0:T(1,128)} %broadcast_in_dim.148), calls=%async_computation.10 | async-start | bytes 262144 | tf_op jit(solution)/shard_map/all_to_all | solution.py:407
  29.7 64.8 %all-to-all-start.11 = ((bf16[256,9,4,128]{3,2,1,0:T(4,128)(2,1)}), bf16[256,9,4,128]{3,2,1,0:T(4,128)(2,1)S(1)}, u32[]{:S(2)}, u32[]{:S(2)}) async-start(bf16[256,9,4,128]{3,2,1,0:T(4,128)(2,1)} %spread_rows.1), calls=%async_computation.11 | async-start | bytes 4718592 | tf_op jit(solution)/shard_map/all_to_all | solution.py:410
